TPU v7x, 32 devices: a whole 2x2x4 slice. The times are simulated.
32 devices in a mesh: groups: 1, ep: 32 (over z, y, x, core).
Axes of the slice: x: 2, y: 2, z: 4, core: 2. Of those that a mesh axis runs over, the one named last changes fastest.
Arguments:
- prefill_rows: bfloat16 [4096, 7168], P(('groups', 'ep')), may hold values from -6 to 6
- proj_weight: bfloat16 [7168, 576], P('ep'), may hold values from -0.0625 to 0.0625
- latent_gain: float32 [512], replicated, may hold values from 0.5 to 1.5
- prefill_position: int32 [4096], P(('groups', 'ep')), may hold values from 0 to 4095
- row_owner: int32 [4096, 1], P(('groups', 'ep')), may hold values from 0 to 31; in each aligned block of 128 rows (0 to 127, 128 to 255, ...) at most 8 rows name the same one
- row_request: int32 [4096], P(('groups', 'ep')), may hold values from 0 to 3
- latent_cache: bfloat16 [128, 256, 576], P(('groups', 'ep')), may hold values from -6 to 6
- cache_len: int32 [128], P(('groups', 'ep')), may hold values from 2 to 256, as said below
- queries: bfloat16 [4, 128, 64, 576], P(None, ('groups', 'ep')), may hold values from -60 to 60
- decode_rows: bfloat16 [4, 128, 7168], P(None, ('groups', 'ep')), may hold values from -6 to 6
- moe_gain: float32 [7168], replicated, may hold values from 0.5 to 1.5
- routes: int32 [4, 128, 2], P(None, ('groups', 'ep')), may hold values from 0 to 3, all different within a row; in each aligned block of 4 rows (0 to 3, 4 to 7, ..., all dimensions but the last counted through in order) at most 2 rows name the same one
- gate_scores: float32 [4, 128, 2], P(None, ('groups', 'ep')), may hold values from 0.1 to 1
- gate_weight: bfloat16 [7168, 4096], P(None, 'ep'), may hold values from -0.0625 to 0.0625
- up_weight: bfloat16 [7168, 4096], P(None, 'ep'), may hold values from -0.0625 to 0.0625
- down_weight: bfloat16 [4096, 7168], P('ep'), may hold values from -0.1875 to 0.1875
Outputs:
- attn_out: bfloat16 [4, 128, 64, 512], P(None, ('groups', 'ep'))
- moe_out: bfloat16 [4, 128, 7168], P(None, ('groups', 'ep'))
Inputs may be any that keep to these rules, and one draw needn't show every extreme that they name: `row_owner`: among the 128 rows of one device, no owner is named more than 8 times, and one owner exactly that often. `routes`: among the 4 tokens of one device at one step, no expert is chosen more than 2 times, and one exactly that often. `cache_len`: some request has exactly 256 rows.
All inputs are finite; a program needn't handle non-finite values.
Results may differ from a plain program's by a relative error of at most 0.0071.
Values may be sent and summed in bfloat16 or wider, within the bound.
A program may use at most 128 MiB of HBM per device.

v0:
```python
import jax
import jax.numpy as jnp
from jax import lax
from jax.sharding import PartitionSpec as P

KV_RANK = 512
MOE_FF = 1024
TOP = 2


NORM_EPS = 1e-06
SOFT_SCALE = 192.0 ** (-0.5)
NEG_FILL = -1e30


def latent_rows(projected, positions, latent_gain):
    compressed = projected[:, :KV_RANK]
    rotary = projected[:, KV_RANK:]
    factor = lax.rsqrt(jnp.mean(compressed * compressed, axis=1, keepdims=True) + NORM_EPS)
    compressed = compressed * factor * latent_gain[None, :]
    half_width = rotary.shape[1] // 2
    frequency = 10000.0 ** (-jnp.arange(half_width, dtype=jnp.float32) / half_width)
    angles = positions.astype(jnp.float32)[:, None] * frequency[None, :]
    cosine = jnp.cos(angles)
    sine_part = jnp.sin(angles)
    first_half = rotary[:, :half_width]
    second_half = rotary[:, half_width:]
    rotated = jnp.concatenate(
        [
            first_half * cosine - second_half * sine_part,
            second_half * cosine + first_half * sine_part,
        ],
        axis=1,
    )
    return jnp.concatenate([compressed, rotated], axis=1).astype(jnp.bfloat16)


def place_rows(destination, local_request, payload, dest_count, capacity):
    dest_ids = jnp.arange(dest_count, dtype=jnp.int32)
    onehot = (destination[:, None] == dest_ids[None, :]).astype(jnp.int32)
    earlier = jnp.cumsum(onehot, axis=0) - onehot
    target = destination * capacity + jnp.sum(earlier * onehot, axis=1)
    select = jnp.arange(dest_count * capacity, dtype=jnp.int32)[:, None] == target[None, :]
    placed = jnp.dot(
        select.astype(jnp.bfloat16), payload, preferred_element_type=jnp.float32
    ).astype(jnp.bfloat16)
    labels = jnp.sum(select.astype(jnp.int32) * (local_request[None, :] + 1), axis=1) - 1
    return (
        placed.reshape(dest_count, capacity, payload.shape[1]),
        labels.reshape(dest_count, capacity),
    )


def attend(queries, cache_rows, lengths, received, labels, own_rows):
    step_count, req_count = (queries.shape[0], queries.shape[1])
    score_cache = (
        jnp.einsum("trhc,rkc->trhk", queries, cache_rows, preferred_element_type=jnp.float32)
        * SOFT_SCALE
    )
    score_recv = (
        jnp.einsum("trhc,mc->trhm", queries, received, preferred_element_type=jnp.float32)
        * SOFT_SCALE
    )
    score_own = (
        jnp.einsum("trhc,src->trhs", queries, own_rows, preferred_element_type=jnp.float32)
        * SOFT_SCALE
    )
    mask_cache = (jnp.arange(cache_rows.shape[1], dtype=jnp.int32)[None, :] < lengths[:, None])[
        None, :, None, :
    ]
    mask_recv = (labels[None, :] == jnp.arange(req_count, dtype=jnp.int32)[:, None])[
        None, :, None, :
    ]
    step_ids = jnp.arange(step_count, dtype=jnp.int32)
    mask_own = (step_ids[None, :] <= step_ids[:, None])[:, None, None, :]
    score_cache = jnp.where(mask_cache, score_cache, NEG_FILL)
    score_recv = jnp.where(mask_recv, score_recv, NEG_FILL)
    score_own = jnp.where(mask_own, score_own, NEG_FILL)
    highest = jnp.maximum(
        jnp.maximum(score_cache.max(axis=-1), score_recv.max(axis=-1)), score_own.max(axis=-1)
    )[..., None]
    exp_cache = jnp.where(mask_cache, jnp.exp(score_cache - highest), 0.0)
    exp_recv = jnp.where(mask_recv, jnp.exp(score_recv - highest), 0.0)
    exp_own = jnp.where(mask_own, jnp.exp(score_own - highest), 0.0)
    denominator = (
        exp_cache.sum(axis=-1, keepdims=True)
        + exp_recv.sum(axis=-1, keepdims=True)
        + exp_own.sum(axis=-1, keepdims=True)
    )
    prob_cache = (exp_cache / denominator).astype(jnp.bfloat16)
    prob_recv = (exp_recv / denominator).astype(jnp.bfloat16)
    prob_own = (exp_own / denominator).astype(jnp.bfloat16)
    result = jnp.einsum(
        "trhk,rkc->trhc", prob_cache, cache_rows[:, :, :KV_RANK], preferred_element_type=jnp.float32
    )
    result = result + jnp.einsum(
        "trhm,mc->trhc", prob_recv, received[:, :KV_RANK], preferred_element_type=jnp.float32
    )
    result = result + jnp.einsum(
        "trhs,src->trhc", prob_own, own_rows[:, :, :KV_RANK], preferred_element_type=jnp.float32
    )
    return result.astype(jnp.bfloat16)


def expert_block(arrived, gate_weight, up_weight, down_weight):
    flattened = arrived.reshape(-1, arrived.shape[2])
    hidden = (
        jax.nn.silu(jnp.dot(flattened, gate_weight, preferred_element_type=jnp.float32))
        * jnp.dot(flattened, up_weight, preferred_element_type=jnp.float32)
    ).astype(jnp.bfloat16)
    return (
        jnp.dot(hidden, down_weight, preferred_element_type=jnp.float32)
        .astype(jnp.bfloat16)
        .reshape(arrived.shape)
    )


def pack_step(normed_step, routes_step, gates_step, expert_count, capacity, split_count):
    chosen = routes_step.reshape(-1)
    onehot = (chosen[:, None] == jnp.arange(expert_count, dtype=jnp.int32)[None, :]).astype(
        jnp.int32
    )
    earlier = jnp.cumsum(onehot, axis=0) - onehot
    target = chosen * capacity + jnp.sum(earlier * onehot, axis=1)
    select = jnp.arange(expert_count * capacity, dtype=jnp.int32)[:, None] == target[None, :]
    source = jnp.repeat(normed_step, TOP, axis=0)
    filled = jnp.dot(
        select.astype(jnp.bfloat16), source, preferred_element_type=jnp.float32
    ).astype(jnp.bfloat16)
    weighting = jnp.where(select, gates_step.reshape(-1)[None, :], 0.0)
    mixing = weighting.reshape(expert_count * capacity, -1, TOP).sum(axis=2).T
    outgoing = jnp.repeat(filled.reshape(expert_count, capacity, -1), split_count, axis=0)
    return (outgoing, mixing)


def shards(
    prefill_rows,
    proj_weight,
    latent_gain,
    prefill_position,
    row_owner,
    row_request,
    latent_cache,
    cache_len,
    queries,
    decode_rows,
    moe_gain,
    routes,
    gate_scores,
    gate_weight,
    up_weight,
    down_weight,
):
    ep_count = lax.axis_size("ep")
    pre_count = prefill_rows.shape[0]
    step_count, req_count, width = (
        decode_rows.shape[0],
        decode_rows.shape[1],
        decode_rows.shape[2],
    )
    latent_width = proj_weight.shape[1]
    all_rows = jnp.concatenate(
        [prefill_rows, decode_rows.reshape(step_count * req_count, width)], axis=0
    )
    projected = jnp.dot(
        all_rows,
        lax.all_gather(proj_weight, "ep", axis=0, tiled=True),
        preferred_element_type=jnp.float32,
    )
    decode_position = (
        cache_len[None, :] + jnp.arange(step_count, dtype=jnp.int32)[:, None]
    ).reshape(-1)
    positions = jnp.concatenate([prefill_position, decode_position], axis=0)
    latent = latent_rows(projected, positions, latent_gain)
    prefill_latent = latent[:pre_count]
    own_rows = latent[pre_count:].reshape(step_count, req_count, latent_width)
    send_cap = max(2, 2 * pre_count // ep_count)
    placed, labels = place_rows(row_owner[:, 0], row_request, prefill_latent, ep_count, send_cap)
    received, received_labels = (
        lax.all_to_all(placed, "ep", split_axis=0, concat_axis=0, tiled=True),
        lax.all_to_all(labels, "ep", split_axis=0, concat_axis=0, tiled=True),
    )
    attn_out = attend(
        queries,
        latent_cache,
        cache_len,
        received.reshape(-1, latent_width),
        received_labels.reshape(-1),
        own_rows,
    )
    token_rows = decode_rows.astype(jnp.float32)
    factor = lax.rsqrt(jnp.mean(token_rows * token_rows, axis=2, keepdims=True) + NORM_EPS)
    normed = (token_rows * factor * moe_gain[None, None, :]).astype(jnp.bfloat16)
    hidden_dev = gate_weight.shape[1]
    split_count = MOE_FF // hidden_dev
    expert_count = ep_count // split_count
    capacity = max(2, req_count * TOP // expert_count)
    packed = [
        pack_step(
            normed[step_at],
            routes[step_at],
            gate_scores[step_at],
            expert_count,
            capacity,
            split_count,
        )
        for step_at in range(step_count)
    ]
    outputs = []
    for step_at in range(step_count):
        returned = lax.all_to_all(
            expert_block(
                lax.all_to_all(packed[step_at][0], "ep", split_axis=0, concat_axis=0, tiled=True),
                gate_weight,
                up_weight,
                down_weight,
            ),
            "ep",
            split_axis=0,
            concat_axis=0,
            tiled=True,
        )
        expert_rows = jnp.sum(
            returned.reshape(expert_count, split_count, -1, width).astype(jnp.float32), axis=1
        ).reshape(expert_count * capacity, width)
        outputs.append(
            jnp.dot(
                packed[step_at][1],
                expert_rows,
                precision=lax.Precision.HIGHEST,
                preferred_element_type=jnp.float32,
            )
        )
    moe_out = jnp.stack(outputs, axis=0).astype(jnp.bfloat16)
    return (attn_out, moe_out)


def solution(mesh):
    in_specs = (
        P(("groups", "ep"), None),
        P("ep", None),
        P(),
        P(("groups", "ep")),
        P(("groups", "ep"), None),
        P(("groups", "ep")),
        P(("groups", "ep"), None, None),
        P(("groups", "ep")),
        P(None, ("groups", "ep"), None, None),
        P(None, ("groups", "ep"), None),
        P(),
        P(None, ("groups", "ep"), None),
        P(None, ("groups", "ep"), None),
        P(None, "ep"),
        P(None, "ep"),
        P("ep", None),
    )
    out_specs = (P(None, ("groups", "ep"), None, None), P(None, ("groups", "ep"), None))
    return jax.shard_map(shards, mesh=mesh, in_specs=in_specs, out_specs=out_specs, check_vma=False)
```

profile of v0, /device:TPU:0, one launch (start us, length us, event | category | flops | bytes accessed | tf_op | source)
XLA Modules:
  0.0 323.4 jit_solution(7422451889094323637)
XLA Ops:
  11.2 7.3 %all-to-all-start = ((s32[32,1,8]{2,1,0:T(1,128)}), s32[32,1,8]{2,1,0:T(1,128)S(1)}, u32[]{:S(2)}, u32[]{:S(2)}) async-start(s32[32,1,8]{2,1,0:T(1,128)} %bitcast.4), calls=%async_computation | async-start | bytes 32768 | tf_op jit(solution)/shard_map/all_to_all | solution.py:181
  22.4 3.2 all-to-all-done
  25.6 1.4 broadcast_in_dim.175
  27.0 2.6 all-to-all-start.8
  30.4 35.9 %all-to-all-done.8 = bf16[32,2,7168]{2,1,0:T(2,128)(2,1)S(1)} async-done(((bf16[32,2,7168]{2,1,0:T(2,128)(2,1)}), bf16[32,2,7168]{2,1,0:T(2,128)(2,1)S(1)}, u32[]{:S(2)}, u32[]{:S(2)}) %all-to-all-start.8) | async-done | bytes 917536 | tf_op jit(solution)/shard_map/all_to_all | solution.py:213
  66.3 1.4 broadcast_in_dim.171
  67.7 4.2 %all-to-all-start.6 = ((bf16[32,2,7168]{2,1,0:T(2,128)(2,1)}), bf16[32,2,7168]{2,1,0:T(2,128)(2,1)}, u32[]{:S(2)}, u32[]{:S(2)}) async-start(bf16[32,2,7168]{2,1,0:T(2,128)(2,1)} %bitcast.144), calls=%async_computation.6 | async-start | bytes 1835008 | tf_op jit(solution)/shard_map/all_to_all | solution.py:213
  72.6 44.7 %all-to-all-done.6 = bf16[32,2,7168]{2,1,0:T(2,128)(2,1)} async-done(((bf16[32,2,7168]{2,1,0:T(2,128)(2,1)}), bf16[32,2,7168]{2,1,0:T(2,128)(2,1)}, u32[]{:S(2)}, u32[]{:S(2)}) %all-to-all-start.6) | async-done | bytes 917536 | tf_op jit(solution)/shard_map/all_to_all | solution.py:213
  117.3 1.4 broadcast_in_dim.167
  118.7 2.8 all-to-all-start.4
  122.3 22.7 %all-to-all-done.4 = bf16[32,2,7168]{2,1,0:T(2,128)(2,1)S(1)} async-done(((bf16[32,2,7168]{2,1,0:T(2,128)(2,1)}), bf16[32,2,7168]{2,1,0:T(2,128)(2,1)S(1)}, u32[]{:S(2)}, u32[]{:S(2)}) %all-to-all-start.4) | async-done | bytes 917536 | tf_op jit(solution)/shard_map/all_to_all | solution.py:213
  144.9 1.4 broadcast_in_dim.163
  146.4 3.7 %all-to-all-start.2 = ((bf16[32,2,7168]{2,1,0:T(2,128)(2,1)}), bf16[32,2,7168]{2,1,0:T(2,128)(2,1)}, u32[]{:S(2)}, u32[]{:S(2)}) async-start(bf16[32,2,7168]{2,1,0:T(2,128)(2,1)} %bitcast.145), calls=%async_computation.2 | async-start | bytes 1835008 | tf_op jit(solution)/shard_map/all_to_all | solution.py:213
  150.1 2.5 reshape.380
  152.6 2.0 fusion.106
  154.5 3.2 %convolution_convert_fusion = bf16[64,7168]{1,0:T(8,128)(2,1)} fusion(bf16[128,7168]{1,0:T(8,128)(2,1)S(1)} %copy-done, bf16[64,7168]{1,0:T(8,128)(2,1)S(1)} %reshape.380, bf16[7168,128]{1,0:T(8,128)(2,1)} %param.30, f32[64,128]{1,0:T(8,128)S(1)} %fusion.106), kind=kOutput, calls=%fused_computation | convolution fusion | flops 235388928 | bytes 5537792 | tf_op jit(solution)/shard_map/dot_general | solution.py:112
  157.8 3.1 reshape.381
  160.9 12.6 %all-to-all-done.2 = bf16[32,2,7168]{2,1,0:T(2,128)(2,1)} async-done(((bf16[32,2,7168]{2,1,0:T(2,128)(2,1)}), bf16[32,2,7168]{2,1,0:T(2,128)(2,1)}, u32[]{:S(2)}, u32[]{:S(2)}) %all-to-all-start.2) | async-done | bytes 917536 | tf_op jit(solution)/shard_map/all_to_all | solution.py:213
  173.5 3.9 %all-to-all-start.9 = ((bf16[32,2,7168]{2,1,0:T(2,128)(2,1)}), bf16[32,2,7168]{2,1,0:T(2,128)(2,1)}, u32[]{:S(2)}, u32[]{:S(2)}) async-start(bf16[32,2,7168]{2,1,0:T(2,128)(2,1)} %reshape.381), calls=%async_computation.9 | async-start | bytes 1835008 | tf_op jit(solution)/shard_map/all_to_all | solution.py:211
  177.4 2.5 reshape.374
  179.9 2.0 fusion.105
  181.9 3.2 %convolution_convert_fusion.1 = bf16[64,7168]{1,0:T(8,128)(2,1)} fusion(bf16[128,7168]{1,0:T(8,128)(2,1)S(1)} %copy-done, bf16[64,7168]{1,0:T(8,128)(2,1)S(1)} %reshape.374, bf16[7168,128]{1,0:T(8,128)(2,1)} %param.30, f32[64,128]{1,0:T(8,128)S(1)} %fusion.105), kind=kOutput, calls=%fused_computation.1 | convolution fusion | flops 235388928 | bytes 5537792 | tf_op jit(solution)/shard_map/dot_general | solution.py:112
  185.1 3.1 reshape.375
  188.2 12.5 %all-to-all-done.9 = bf16[32,2,7168]{2,1,0:T(2,128)(2,1)} async-done(((bf16[32,2,7168]{2,1,0:T(2,128)(2,1)}), bf16[32,2,7168]{2,1,0:T(2,128)(2,1)}, u32[]{:S(2)}, u32[]{:S(2)}) %all-to-all-start.9) | async-done | bytes 917536 | tf_op jit(solution)/shard_map/all_to_all | solution.py:211
  200.7 3.7 %all-to-all-start.7 = ((bf16[32,2,7168]{2,1,0:T(2,128)(2,1)}), bf16[32,2,7168]{2,1,0:T(2,128)(2,1)}, u32[]{:S(2)}, u32[]{:S(2)}) async-start(bf16[32,2,7168]{2,1,0:T(2,128)(2,1)} %reshape.375), calls=%async_computation.7 | async-start | bytes 1835008 | tf_op jit(solution)/shard_map/all_to_all | solution.py:211
  204.4 2.5 reshape.368
  206.9 2.0 fusion.104
  208.9 3.2 %convolution_convert_fusion.2 = bf16[64,7168]{1,0:T(8,128)(2,1)} fusion(bf16[128,7168]{1,0:T(8,128)(2,1)S(1)} %copy-done, bf16[64,7168]{1,0:T(8,128)(2,1)S(1)} %reshape.368, bf16[7168,128]{1,0:T(8,128)(2,1)} %param.30, f32[64,128]{1,0:T(8,128)S(1)} %fusion.104), kind=kOutput, calls=%fused_computation.2 | convolution fusion | flops 235388928 | bytes 5537792 | tf_op jit(solution)/shard_map/dot_general | solution.py:112
  212.1 3.1 reshape.369
  215.3 12.6 %all-to-all-done.7 = bf16[32,2,7168]{2,1,0:T(2,128)(2,1)} async-done(((bf16[32,2,7168]{2,1,0:T(2,128)(2,1)}), bf16[32,2,7168]{2,1,0:T(2,128)(2,1)}, u32[]{:S(2)}, u32[]{:S(2)}) %all-to-all-start.7) | async-done | bytes 917536 | tf_op jit(solution)/shard_map/all_to_all | solution.py:211
  227.8 3.7 %all-to-all-start.5 = ((bf16[32,2,7168]{2,1,0:T(2,128)(2,1)}), bf16[32,2,7168]{2,1,0:T(2,128)(2,1)}, u32[]{:S(2)}, u32[]{:S(2)}) async-start(bf16[32,2,7168]{2,1,0:T(2,128)(2,1)} %reshape.369), calls=%async_computation.5 | async-start | bytes 1835008 | tf_op jit(solution)/shard_map/all_to_all | solution.py:211
  233.2 2.5 reshape.362
  235.7 2.0 fusion.103
  237.7 3.2 %convolution_convert_fusion.3 = bf16[64,7168]{1,0:T(8,128)(2,1)} fusion(bf16[128,7168]{1,0:T(8,128)(2,1)S(1)} %copy-done, bf16[64,7168]{1,0:T(8,128)(2,1)S(1)} %reshape.362, bf16[7168,128]{1,0:T(8,128)(2,1)} %param.30, f32[64,128]{1,0:T(8,128)S(1)} %fusion.103), kind=kOutput, calls=%fused_computation.3 | convolution fusion | flops 235388928 | bytes 5537792 | tf_op jit(solution)/shard_map/dot_general | solution.py:112
  240.9 3.1 reshape.363
  244.0 11.0 %all-to-all-done.5 = bf16[32,2,7168]{2,1,0:T(2,128)(2,1)} async-done(((bf16[32,2,7168]{2,1,0:T(2,128)(2,1)}), bf16[32,2,7168]{2,1,0:T(2,128)(2,1)}, u32[]{:S(2)}, u32[]{:S(2)}) %all-to-all-start.5) | async-done | bytes 917536 | tf_op jit(solution)/shard_map/all_to_all | solution.py:211
  255.0 3.8 %all-to-all-start.3 = ((bf16[32,2,7168]{2,1,0:T(2,128)(2,1)}), bf16[32,2,7168]{2,1,0:T(2,128)(2,1)S(1)}, u32[]{:S(2)}, u32[]{:S(2)}) async-start(bf16[32,2,7168]{2,1,0:T(2,128)(2,1)} %reshape.363), calls=%async_computation.3 | async-start | bytes 1835008 | tf_op jit(solution)/shard_map/all_to_all | solution.py:211
  259.1 3.2 %fusion.101 = (f32[4,4,64]{2,0,1:T(4,128)S(1)}, f32[4,4,64,256]{3,2,0,1:T(8,128)}) fusion(bf16[4,4,64,576]{3,2,1,0:T(8,128)(2,1)} %param.24, bf16[4,256,576]{1,2,0:T(8,128)(2,1)} %param.22, pred[4,256]{1,0:T(4,128)(4,1)S(1)} %iota_compare_fusion.12), kind=kOutput, calls=%fused_computation.197 | convolution fusion | flops 302775296 | bytes 3412992 | tf_op jit(solution)/shard_map/trhc,rkc->trhk/dot_general | solution.py:57
  263.8 2.1 convert_reduce_fusion
  266.0 2.1 convert_reduce_fusion.1
  268.3 2.8 convert_reduce_fusion.2
  272.2 9.9 %all-to-all-done.3 = bf16[32,2,7168]{2,1,0:T(2,128)(2,1)S(1)} async-done(((bf16[32,2,7168]{2,1,0:T(2,128)(2,1)}), bf16[32,2,7168]{2,1,0:T(2,128)(2,1)S(1)}, u32[]{:S(2)}, u32[]{:S(2)}) %all-to-all-start.3) | async-done | bytes 917536 | tf_op jit(solution)/shard_map/all_to_all | solution.py:211
  282.1 1.5 convert_reduce_fusion.3
  286.1 6.0 %fusion.5 = f32[144,576]{1,0:T(8,128)S(1)} fusion(bf16[7168,576]{1,0:T(8,128)(2,1)} %all-gather.2.cloned.1.call-done, bf16[16,7168]{1,0:T(8,128)(2,1)} %reshape.355, bf16[128,7168]{1,0:T(8,128)(2,1)} %param.16), kind=kOutput, calls=%fused_computation.19 | convolution fusion | flops 1193213952 | bytes 10653696 | tf_op jit(solution)/shard_map/dot_general | solution.py:165
  294.3 3.9 %all-to-all-start.1 = ((bf16[32,8,576]{2,1,0:T(8,128)(2,1)}), bf16[32,8,576]{2,1,0:T(8,128)(2,1)S(1)}, u32[]{:S(2)}, u32[]{:S(2)}) async-start(bf16[32,8,576]{2,1,0:T(8,128)(2,1)} %bitcast.5), calls=%async_computation.1 | async-start | bytes 655360 | tf_op jit(solution)/shard_map/all_to_all | solution.py:180
  299.2 2.1 fusion.100
  301.3 8.7 %all-to-all-done.1 = bf16[32,8,576]{2,1,0:T(8,128)(2,1)S(1)} async-done(((bf16[32,8,576]{2,1,0:T(8,128)(2,1)}), bf16[32,8,576]{2,1,0:T(8,128)(2,1)S(1)}, u32[]{:S(2)}, u32[]{:S(2)}) %all-to-all-start.1) | async-done | bytes 294944 | tf_op jit(solution)/shard_map/all_to_all | solution.py:180
  309.9 2.0 fusion.102
  (132 shorter events, 24.7 us)
Async XLA Ops:
  7.2 147.4 %copy-start = (bf16[128,7168]{1,0:T(8,128)(2,1)S(1)}, bf16[128,7168]{1,0:T(8,128)(2,1)}, u32[]{:S(2)}) copy-start(bf16[128,7168]{1,0:T(8,128)(2,1)} %param.31) | copy-start | bytes 5505028
  7.2 278.9 %all-gather.2.cloned.1.call-start = ((), (), s32[]{:S(2)}) async-start(), calls=%async_computation.10 | async-start | bytes 9461760 | tf_op jit(solution)/shard_map/all_gather | solution.py:167
  11.2 14.4 %all-to-all-start = ((s32[32,1,8]{2,1,0:T(1,128)}), s32[32,1,8]{2,1,0:T(1,128)S(1)}, u32[]{:S(2)}, u32[]{:S(2)}) async-start(s32[32,1,8]{2,1,0:T(1,128)} %bitcast.4), calls=%async_computation | async-start | bytes 32768 | tf_op jit(solution)/shard_map/all_to_all | solution.py:181
  27.0 39.3 %all-to-all-start.8 = ((bf16[32,2,7168]{2,1,0:T(2,128)(2,1)}), bf16[32,2,7168]{2,1,0:T(2,128)(2,1)S(1)}, u32[]{:S(2)}, u32[]{:S(2)}) async-start(bf16[32,2,7168]{2,1,0:T(2,128)(2,1)} %bitcast.143), calls=%async_computation.8 | async-start | bytes 1835008 | tf_op jit(solution)/shard_map/all_to_all | solution.py:213
  66.3 6.3 %copy-start.1 = (bf16[32,2,7168]{2,1,0:T(2,128)(2,1)}, bf16[32,2,7168]{2,1,0:T(2,128)(2,1)S(1)}, u32[]{:S(2)}) copy-start(bf16[32,2,7168]{2,1,0:T(2,128)(2,1)S(1)} %all-to-all-done.8) | copy-start | bytes 2752516
  67.7 49.6 %all-to-all-start.6 = ((bf16[32,2,7168]{2,1,0:T(2,128)(2,1)}), bf16[32,2,7168]{2,1,0:T(2,128)(2,1)}, u32[]{:S(2)}, u32[]{:S(2)}) async-start(bf16[32,2,7168]{2,1,0:T(2,128)(2,1)} %bitcast.144), calls=%async_computation.6 | async-start | bytes 1835008 | tf_op jit(solution)/shard_map/all_to_all | solution.py:213
  118.7 26.3 %all-to-all-start.4 = ((bf16[32,2,7168]{2,1,0:T(2,128)(2,1)}), bf16[32,2,7168]{2,1,0:T(2,128)(2,1)S(1)}, u32[]{:S(2)}, u32[]{:S(2)}) async-start(bf16[32,2,7168]{2,1,0:T(2,128)(2,1)} %bitcast.142), calls=%async_computation.4 | async-start | bytes 1835008 | tf_op jit(solution)/shard_map/all_to_all | solution.py:213
  144.9 1.4 copy-start.2
  146.4 27.2 %all-to-all-start.2 = ((bf16[32,2,7168]{2,1,0:T(2,128)(2,1)}), bf16[32,2,7168]{2,1,0:T(2,128)(2,1)}, u32[]{:S(2)}, u32[]{:S(2)}) async-start(bf16[32,2,7168]{2,1,0:T(2,128)(2,1)} %bitcast.145), calls=%async_computation.2 | async-start | bytes 1835008 | tf_op jit(solution)/shard_map/all_to_all | solution.py:213
  173.5 27.2 %all-to-all-start.9 = ((bf16[32,2,7168]{2,1,0:T(2,128)(2,1)}), bf16[32,2,7168]{2,1,0:T(2,128)(2,1)}, u32[]{:S(2)}, u32[]{:S(2)}) async-start(bf16[32,2,7168]{2,1,0:T(2,128)(2,1)} %reshape.381), calls=%async_computation.9 | async-start | bytes 1835008 | tf_op jit(solution)/shard_map/all_to_all | solution.py:211
  200.7 27.2 %all-to-all-start.7 = ((bf16[32,2,7168]{2,1,0:T(2,128)(2,1)}), bf16[32,2,7168]{2,1,0:T(2,128)(2,1)}, u32[]{:S(2)}, u32[]{:S(2)}) async-start(bf16[32,2,7168]{2,1,0:T(2,128)(2,1)} %reshape.375), calls=%async_computation.7 | async-start | bytes 1835008 | tf_op jit(solution)/shard_map/all_to_all | solution.py:211
  212.1 19.5 %copy-start.3 = (bf16[4,4,7168]{2,1,0:T(4,128)(2,1)S(1)}, bf16[4,4,7168]{2,1,0:T(4,128)(2,1)}, u32[]{:S(2)}) copy-start(bf16[4,4,7168]{2,1,0:T(4,128)(2,1)} %param.25) | copy-start | bytes 688132
  212.1 20.6 %copy-start.8 = (s32[4]{0:T(128)S(1)}, s32[4]{0:T(128)}, u32[]{:S(2)}) copy-start(s32[4]{0:T(128)} %param.23) | copy-start | bytes 52
  212.1 21.0 %copy-start.9 = (s32[128]{0:T(128)S(1)}, s32[128]{0:T(128)}, u32[]{:S(2)}) copy-start(s32[128]{0:T(128)} %param.19) | copy-start | bytes 1540
  212.1 21.1 %copy-start.6 = (f32[4,4,2]{1,2,0:T(2,128)S(1)}, f32[4,4,2]{1,2,0:T(2,128)}, u32[]{:S(2)}) copy-start(f32[4,4,2]{1,2,0:T(2,128)} %param.28) | copy-start | bytes 388
  212.1 21.1 %copy-start.5 = (s32[4,4,2]{1,2,0:T(2,128)S(1)}, s32[4,4,2]{1,2,0:T(2,128)}, u32[]{:S(2)}) copy-start(s32[4,4,2]{1,2,0:T(2,128)} %param.27) | copy-start | bytes 388
  227.8 27.2 %all-to-all-start.5 = ((bf16[32,2,7168]{2,1,0:T(2,128)(2,1)}), bf16[32,2,7168]{2,1,0:T(2,128)(2,1)}, u32[]{:S(2)}, u32[]{:S(2)}) async-start(bf16[32,2,7168]{2,1,0:T(2,128)(2,1)} %reshape.369), calls=%async_computation.5 | async-start | bytes 1835008 | tf_op jit(solution)/shard_map/all_to_all | solution.py:211
  255.0 27.1 %all-to-all-start.3 = ((bf16[32,2,7168]{2,1,0:T(2,128)(2,1)}), bf16[32,2,7168]{2,1,0:T(2,128)(2,1)S(1)}, u32[]{:S(2)}, u32[]{:S(2)}) async-start(bf16[32,2,7168]{2,1,0:T(2,128)(2,1)} %reshape.363), calls=%async_computation.3 | async-start | bytes 1835008 | tf_op jit(solution)/shard_map/all_to_all | solution.py:211
  286.0 6.9 %copy-start.7 = (f32[512]{0:T(512)S(1)}, f32[512]{0:T(512)}, u32[]{:S(2)}) copy-start(f32[512]{0:T(512)} %param.18) | copy-start | bytes 6148
  294.3 15.6 %all-to-all-start.1 = ((bf16[32,8,576]{2,1,0:T(8,128)(2,1)}), bf16[32,8,576]{2,1,0:T(8,128)(2,1)S(1)}, u32[]{:S(2)}, u32[]{:S(2)}) async-start(bf16[32,8,576]{2,1,0:T(8,128)(2,1)} %bitcast.5), calls=%async_computation.1 | async-start | bytes 655360 | tf_op jit(solution)/shard_map/all_to_all | solution.py:180
  301.2 10.8 %copy-start.4 = (f32[4,4,64,256]{3,2,0,1:T(8,128)S(1)}, f32[4,4,64,256]{3,2,0,1:T(8,128)}, u32[]{:S(2)}) copy-start(f32[4,4,64,256]{3,2,0,1:T(8,128)} %get-tuple-element.37) | copy-start | bytes 3145732
  313.6 1.3 copy-start.10
Sparse Core Ops, SparseCore 0:
  10.9 110.1 all-gather.1
where the time goes:
time: 325 us; the launch traced here: 323 us
  waiting for transfers between devices  174 us (54%)
  starting transfers between devices  39.8 us (12%)
  local copies, waits for them, and re-layouts  38.7 us (12%)
  matrix products  38.1 us (12%)
  other arithmetic  17.7 us (5%)
  between operations  14.6 us (4%)
    all_to_all x4, waiting for transfers between devices, shards(): lax.all_to_all(packed[step_at][0], 'ep', split_axis=0, concat_axis=0, til...  116 us
    all_to_all x4, waiting for transfers between devices, shards(): lax.all_to_all(expert_block(lax.all_to_all(packed[step_at][0], 'ep', spli...  45.9 us
    all_to_all x4, starting transfers between devices, shards(): lax.all_to_all(expert_block(lax.all_to_all(packed[step_at][0], 'ep', spli...  15.2 us
    all_to_all x4, starting transfers between devices, shards(): lax.all_to_all(packed[step_at][0], 'ep', split_axis=0, concat_axis=0, til...  13.4 us
    dot_general x4, matrix products, expert_block(): jnp.dot(hidden, down_weight, preferred_element_type=jnp.float32)  13 us
    reshape x4, local copies, waits for them, and re-layouts, expert_block(): return jnp.dot(hidden, down_weight, preferred_element_type=jnp.float32).a...  12.4 us
    reshape x4, local copies, waits for them, and re-layouts, expert_block(): flattened = arrived.reshape(-1, arrived.shape[2])  9.91 us
    all_to_all x1, waiting for transfers between devices, shards(): lax.all_to_all(placed, 'ep', split_axis=0, concat_axis=0, tiled=True)  8.66 us
  transfers between devices with their start and end apart: 11, of which 10 were waited for; matrix products, arithmetic and copies ran while one was open for 25% of the time, Pallas kernels for 0%

commit v1 on v0

v1 whole, which is shorter than its diff:
```python
import functools

import jax
import jax.numpy as jnp
from jax import lax
from jax.experimental import pallas as pl
from jax.experimental.pallas import tpu as pltpu
from jax.sharding import PartitionSpec as P

KV_RANK = 512
MOE_FF = 1024
TOP = 2


NORM_EPS = 1e-06
SOFT_SCALE = 192.0 ** (-0.5)
NEG_FILL = -1e30


def latent_rows(projected, positions, latent_gain):
    compressed = projected[:, :KV_RANK]
    rotary = projected[:, KV_RANK:]
    factor = lax.rsqrt(jnp.mean(compressed * compressed, axis=1, keepdims=True) + NORM_EPS)
    compressed = compressed * factor * latent_gain[None, :]
    half_width = rotary.shape[1] // 2
    frequency = 10000.0 ** (-jnp.arange(half_width, dtype=jnp.float32) / half_width)
    angles = positions.astype(jnp.float32)[:, None] * frequency[None, :]
    cosine = jnp.cos(angles)
    sine_part = jnp.sin(angles)
    first_half = rotary[:, :half_width]
    second_half = rotary[:, half_width:]
    rotated = jnp.concatenate(
        [
            first_half * cosine - second_half * sine_part,
            second_half * cosine + first_half * sine_part,
        ],
        axis=1,
    )
    return jnp.concatenate([compressed, rotated], axis=1).astype(jnp.bfloat16)


def attend(queries, cache_rows, lengths, received, labels, own_rows):
    step_count, req_count = (queries.shape[0], queries.shape[1])
    score_cache = (
        jnp.einsum("trhc,rkc->trhk", queries, cache_rows, preferred_element_type=jnp.float32)
        * SOFT_SCALE
    )
    score_recv = (
        jnp.einsum("trhc,mc->trhm", queries, received, preferred_element_type=jnp.float32)
        * SOFT_SCALE
    )
    score_own = (
        jnp.einsum("trhc,src->trhs", queries, own_rows, preferred_element_type=jnp.float32)
        * SOFT_SCALE
    )
    mask_cache = (jnp.arange(cache_rows.shape[1], dtype=jnp.int32)[None, :] < lengths[:, None])[
        None, :, None, :
    ]
    mask_recv = (labels[None, :] == jnp.arange(req_count, dtype=jnp.int32)[:, None])[
        None, :, None, :
    ]
    step_ids = jnp.arange(step_count, dtype=jnp.int32)
    mask_own = (step_ids[None, :] <= step_ids[:, None])[:, None, None, :]
    score_cache = jnp.where(mask_cache, score_cache, NEG_FILL)
    score_recv = jnp.where(mask_recv, score_recv, NEG_FILL)
    score_own = jnp.where(mask_own, score_own, NEG_FILL)
    highest = jnp.maximum(
        jnp.maximum(score_cache.max(axis=-1), score_recv.max(axis=-1)), score_own.max(axis=-1)
    )[..., None]
    exp_cache = jnp.where(mask_cache, jnp.exp(score_cache - highest), 0.0)
    exp_recv = jnp.where(mask_recv, jnp.exp(score_recv - highest), 0.0)
    exp_own = jnp.where(mask_own, jnp.exp(score_own - highest), 0.0)
    denominator = (
        exp_cache.sum(axis=-1, keepdims=True)
        + exp_recv.sum(axis=-1, keepdims=True)
        + exp_own.sum(axis=-1, keepdims=True)
    )
    prob_cache = (exp_cache / denominator).astype(jnp.bfloat16)
    prob_recv = (exp_recv / denominator).astype(jnp.bfloat16)
    prob_own = (exp_own / denominator).astype(jnp.bfloat16)
    result = jnp.einsum(
        "trhk,rkc->trhc", prob_cache, cache_rows[:, :, :KV_RANK], preferred_element_type=jnp.float32
    )
    result = result + jnp.einsum(
        "trhm,mc->trhc", prob_recv, received[:, :KV_RANK], preferred_element_type=jnp.float32
    )
    result = result + jnp.einsum(
        "trhs,src->trhc", prob_own, own_rows[:, :, :KV_RANK], preferred_element_type=jnp.float32
    )
    return result.astype(jnp.bfloat16)


PLANE = 8
SLAB = 16
TILE = 512


def place_rows(destination, payload, dest_count, capacity):
    dest_ids = jnp.arange(dest_count, dtype=jnp.int32)
    onehot = (destination[:, None] == dest_ids[None, :]).astype(jnp.int32)
    earlier = jnp.cumsum(onehot, axis=0) - onehot
    target = destination * capacity + jnp.sum(earlier * onehot, axis=1)
    select = jnp.arange(dest_count * capacity, dtype=jnp.int32)[:, None] == target[None, :]
    placed = jnp.dot(
        select.astype(jnp.bfloat16), payload, preferred_element_type=jnp.float32
    ).astype(jnp.bfloat16)
    return placed.reshape(dest_count, capacity, payload.shape[1])


def exchange_kernel(
    expert_count,
    w_ref, tok_ref, pre_hbm, dec_ref, gate_hbm, up_hbm, down_hbm,
    proj_ref, back_ref,
    weight, tokens, pre, gate, up, down, accum, hidden, part,
    from_sib, from_a, from_b, sum_a, sum_d, own_sum, sum_b, total, back,
    zs, zr, ps, pr, local, ss, sr, as_, ar, bs, br, fs, fr,
):
    E = expert_count
    me = lax.axis_index("ep")
    e0 = me // PLANE
    j = me % PLANE
    b0, b1, b2 = j % 2, (j // 2) % 2, j // 4
    dx = 2 - 4 * b1
    dy = 4 - 8 * b2
    ds = 1 - 2 * b0
    da = dx * (1 - b0) + dy * b0
    db = dx * b0 + dy * (1 - b0)
    jS, jA, jB, jD = j + ds, j + da, j + db, j + dx + dy
    sA, sB, sD = jS + db, jS + da, jS + dx + dy
    base = e0 * PLANE
    half = tok_ref.shape[2]

    def remote(src, dst, send, recv, device):
        return pltpu.make_async_remote_copy(
            src_ref=src, dst_ref=dst, send_sem=send, recv_sem=recv,
            device_id={"ep": device}, device_id_type=pl.DeviceIdType.MESH,
        )

    loads = [
        pltpu.make_async_copy(w_ref, weight.at[e0, j], local.at[0]),
        pltpu.make_async_copy(tok_ref.at[e0], tokens.at[e0, j], local.at[1]),
        pltpu.make_async_copy(gate_hbm, gate, local.at[2]),
        pltpu.make_async_copy(up_hbm, up, local.at[3]),
        pltpu.make_async_copy(pre_hbm, pre, local.at[4]),
        pltpu.make_async_copy(down_hbm, down, local.at[5]),
    ]
    for load in loads:
        load.start()

    barrier = pltpu.get_barrier_semaphore()
    for k in range(1, E):
        pl.semaphore_signal(
            barrier, inc=1, device_id={"ep": ((e0 + k) % E) * PLANE + j},
            device_id_type=pl.DeviceIdType.MESH,
        )
    for peer in (jS, jA, jB):
        pl.semaphore_signal(
            barrier, inc=1, device_id={"ep": base + peer},
            device_id_type=pl.DeviceIdType.MESH,
        )
    pl.semaphore_wait(barrier, E - 1 + 3)

    def column_send(kind, e):
        source = tok_ref.at[e] if kind == 0 else w_ref
        buffer = tokens if kind == 0 else weight
        return remote(
            source, buffer.at[e0, j], zs.at[kind, e], zr.at[kind, e0], e * PLANE + j
        )

    def column_recv(kind, e):
        source = tok_ref.at[e] if kind == 0 else w_ref
        buffer = tokens if kind == 0 else weight
        return remote(
            source, buffer.at[e, j], zs.at[kind, e], zr.at[kind, e], e * PLANE + j
        )

    for k in range(1, E):
        e = (e0 + k) % E
        column_send(0, e).start()
        column_send(1, e).start()
    loads[0].wait()
    loads[1].wait()

    def plane_send(kind, e, which):
        buffer = tokens if kind == 0 else weight
        block = (j, j, j, jA, jA, jB, jD)[which]
        peer = (jA, jB, jS, jB, jS, jS, jS)[which]
        ref = buffer.at[e, block]
        return remote(ref, ref, ps.at[kind, e, which], pr.at[kind, e, which], base + peer)

    def plane_recv(kind, e, which):
        buffer = tokens if kind == 0 else weight
        block = (jA, jB, jS, jD, sA, sB, sD)[which]
        peer = (jA, jB, jS, jB, jS, jS, jS)[which]
        ref = buffer.at[e, block]
        return remote(ref, ref, ps.at[kind, e, which], pr.at[kind, e, which], base + peer)

    def expert_in(e):
        @pl.loop(0, half // TILE)
        def _(t):
            first = pl.multiple_of(t * TILE, TILE)
            second = pl.multiple_of(half + t * TILE, TILE)
            x = tokens[e, :, :, pl.ds(first, TILE)].reshape(PLANE * SLAB, TILE)
            for at, (matrix, start) in enumerate(
                ((gate, first), (gate, second), (up, first), (up, second))
            ):
                product = jnp.dot(
                    x, matrix[pl.ds(start, TILE), :], preferred_element_type=jnp.float32
                )
                accum[at] = jnp.where(t == 0, 0.0, accum[at]) + product

        def joined(at):
            low = accum[at].reshape(PLANE, SLAB, -1)[:, : SLAB // 2]
            high = accum[at + 1].reshape(PLANE, SLAB, -1)[:, SLAB // 2 :]
            return (low + high).reshape(PLANE * SLAB // 2, -1)

        hidden[e] = (jax.nn.silu(joined(0)) * joined(2)).astype(jnp.bfloat16)

    loads[2].wait()
    loads[3].wait()

    @pl.loop(0, E + 3)
    def _(t):
        @pl.when(t < E)
        def _():
            e = (e0 + t) % E
            for kind in (0, 1):
                @pl.when(t > 0)
                def _():
                    column_recv(kind, e).wait_recv()
                for which in (0, 1, 2):
                    plane_send(kind, e, which).start()

        @pl.when((t >= 1) & (t < E + 1))
        def _():
            e = (e0 + t - 1) % E
            for kind in (0, 1):
                plane_recv(kind, e, 0).wait_recv()
                plane_send(kind, e, 3).start()
                plane_send(kind, e, 4).start()
                plane_recv(kind, e, 1).wait_recv()
                plane_send(kind, e, 5).start()

        @pl.when((t >= 2) & (t < E + 2))
        def _():
            e = (e0 + t - 2) % E
            for kind in (0, 1):
                plane_recv(kind, e, 3).wait_recv()
                plane_send(kind, e, 6).start()

        @pl.when(t >= 3)
        def _():
            e = (e0 + t - 3) % E
            for which in (2, 4, 5, 6):
                plane_recv(0, e, which).wait_recv()
            expert_in(e)

    loads[4].wait()
    loads[5].wait()

    def project():
        pre_count = pre.shape[0]
        depth = pre.shape[1] // E

        @pl.loop(0, E)
        def _(e):
            for which in (2, 4, 5, 6):
                plane_recv(1, e, which).wait_recv()

        @pl.loop(0, E)
        def _(e):
            block = weight[e].reshape(depth, -1)
            columns = pl.ds(pl.multiple_of(e * depth, 128), depth)
            for rows, offset in ((pre, 0), (dec_ref, pre_count)):
                place = pl.ds(offset, rows.shape[0])
                product = jnp.dot(
                    rows[:, columns], block, preferred_element_type=jnp.float32
                )
                proj_ref[place, :] = jnp.where(e == 0, 0.0, proj_ref[place, :]) + product

    def sib_send(e, which):
        block = (jS, sA, sB, sD)[which]
        return remote(
            part.at[e, block], from_sib.at[e, which], ss.at[e, which], sr.at[e, which], base + jS
        )

    def a_send(e, which):
        source = (sum_a, sum_d)[which]
        return remote(
            source.at[e], from_a.at[e, which], as_.at[e, which], ar.at[e, which], base + jA
        )

    def b_send(e):
        return remote(sum_b.at[e], from_b.at[e], bs.at[e], br.at[e], base + jB)

    def back_send(e):
        return remote(total.at[e], back.at[e0], fs.at[e], fr.at[e0], e * PLANE + j)

    def back_recv(e):
        return remote(total.at[e], back.at[e], fs.at[e], fr.at[e], e * PLANE + j)

    def wide(ref):
        return ref.astype(jnp.float32)

    @pl.loop(0, E + 3)
    def _(t):
        @pl.when(t < E)
        def _():
            e = (e0 + 1 + t) % E

            @pl.loop(0, half // TILE)
            def _(c):
                first = pl.multiple_of(c * TILE, TILE)
                second = pl.multiple_of(half + c * TILE, TILE)
                low, high = (
                    jnp.dot(
                        hidden[e], down[:, pl.ds(start, TILE)],
                        preferred_element_type=jnp.float32,
                    ).reshape(PLANE, SLAB // 2, TILE)
                    for start in (first, second)
                )
                part[e, :, :, pl.ds(first, TILE)] = jnp.concatenate([low, high], axis=1).astype(
                    jnp.bfloat16
                )

            for which in range(4):
                sib_send(e, which).start()

        @pl.when((t >= 1) & (t < E + 1))
        def _():
            e = (e0 + t) % E
            sib_send(e, 1).wait_recv()
            sum_a[e] = (wide(part[e, jA]) + wide(from_sib[e, 1])).astype(jnp.bfloat16)
            a_send(e, 0).start()
            sib_send(e, 3).wait_recv()
            sum_d[e] = (wide(part[e, jD]) + wide(from_sib[e, 3])).astype(jnp.bfloat16)
            a_send(e, 1).start()

        @pl.when((t >= 2) & (t < E + 2))
        def _():
            e = (e0 + t - 1) % E
            sib_send(e, 0).wait_recv()
            sib_send(e, 2).wait_recv()
            a_send(e, 1).wait_recv()
            sum_b[e] = (
                wide(part[e, jB]) + wide(from_sib[e, 2]) + wide(from_a[e, 1])
            ).astype(jnp.bfloat16)
            b_send(e).start()
            a_send(e, 0).wait_recv()
            own_sum[e] = wide(part[e, j]) + wide(from_sib[e, 0]) + wide(from_a[e, 0])

        @pl.when(t >= 3)
        def _():
            e = (e0 + t - 2) % E
            b_send(e).wait_recv()
            total[e] = (own_sum[e] + wide(from_b[e])).astype(jnp.bfloat16)

            @pl.when(t < E + 2)
            def _():
                back_send(e).start()

        @pl.when(t == 1)
        def _():
            project()

    back_ref[e0] = wide(total[e0])

    @pl.loop(1, E)
    def _(k):
        e = (e0 + k) % E
        back_recv(e).wait_recv()
        back_ref[e] = wide(back[e])

    @pl.loop(0, E)
    def _(e):
        for kind in (0, 1):
            for which in range(7):
                plane_send(kind, e, which).wait_send()
        for which in range(4):
            sib_send(e, which).wait_send()
        a_send(e, 0).wait_send()
        a_send(e, 1).wait_send()
        b_send(e).wait_send()

    @pl.loop(1, E)
    def _(k):
        e = (e0 + k) % E
        column_send(0, e).wait_send()
        column_send(1, e).wait_send()
        back_send(e).wait_send()


def exchange(proj_weight, packed, prefill_rows, decode_flat, gate_weight, up_weight, down_weight):
    E, _, half = packed.shape
    width = 2 * half
    shard, latent_width = proj_weight.shape
    hidden_dev = gate_weight.shape[1]
    rows = prefill_rows.shape[0] + decode_flat.shape[0]
    bf16 = jnp.bfloat16
    block = (E, SLAB, half)
    dma = pltpu.SemaphoreType.DMA
    vmem = pl.BlockSpec(memory_space=pltpu.VMEM)
    hbm = pl.BlockSpec(memory_space=pl.ANY)
    return pl.pallas_call(
        functools.partial(exchange_kernel, E),
        out_shape=(
            jax.ShapeDtypeStruct((rows, latent_width), jnp.float32),
            jax.ShapeDtypeStruct(block, jnp.float32),
        ),
        in_specs=[vmem, vmem, hbm, vmem, hbm, hbm, hbm],
        out_specs=(vmem, vmem),
        scratch_shapes=[
            pltpu.VMEM((E, PLANE, shard, latent_width), bf16),
            pltpu.VMEM((E, PLANE, SLAB, half), bf16),
            pltpu.VMEM(prefill_rows.shape, bf16),
            pltpu.VMEM(gate_weight.shape, bf16),
            pltpu.VMEM(up_weight.shape, bf16),
            pltpu.VMEM(down_weight.shape, bf16),
            pltpu.VMEM((4, PLANE * SLAB, hidden_dev), jnp.float32),
            pltpu.VMEM((E, PLANE * SLAB // 2, hidden_dev), bf16),
            pltpu.VMEM((E, PLANE, SLAB, half), bf16),
            pltpu.VMEM((E, 4, SLAB, half), bf16),
            pltpu.VMEM((E, 2, SLAB, half), bf16),
            pltpu.VMEM(block, bf16),
            pltpu.VMEM(block, bf16),
            pltpu.VMEM(block, bf16),
            pltpu.VMEM(block, jnp.float32),
            pltpu.VMEM(block, bf16),
            pltpu.VMEM(block, bf16),
            pltpu.VMEM(block, bf16),
            dma((2, E)), dma((2, E)), dma((2, E, 7)), dma((2, E, 7)), dma((6,)),
            dma((E, 4)), dma((E, 4)), dma((E, 2)), dma((E, 2)), dma((E,)), dma((E,)),
            dma((E,)), dma((E,)),
        ],
        compiler_params=pltpu.CompilerParams(
            collective_id=0, has_side_effects=True, vmem_limit_bytes=56 * 1024 * 1024
        ),
    )(proj_weight, packed, prefill_rows, decode_flat, gate_weight, up_weight, down_weight)


def pack(normed, routes, gate_scores, expert_count, capacity):
    step_count, req_count, width = normed.shape
    chosen = routes.reshape(step_count, req_count * TOP)
    onehot = (chosen[:, :, None] == jnp.arange(expert_count, dtype=jnp.int32)).astype(jnp.int32)
    earlier = jnp.cumsum(onehot, axis=1) - onehot
    slots = step_count * capacity
    step_ids = jnp.arange(step_count, dtype=jnp.int32)[:, None]
    row = chosen * slots + step_ids * capacity + jnp.sum(earlier * onehot, axis=2)
    row = row.reshape(step_count * req_count, TOP)
    match = row[:, :, None] == jnp.arange(expert_count * slots, dtype=jnp.int32)
    mixing = jnp.sum(jnp.where(match, gate_scores.reshape(-1, TOP)[:, :, None], 0.0), axis=1)
    select = jnp.any(match, axis=1).astype(jnp.bfloat16)
    packed = jnp.einsum(
        "tr,td->rd", select, normed.reshape(-1, width), preferred_element_type=jnp.float32
    ).astype(jnp.bfloat16)
    packed = packed.reshape(expert_count, slots, 2, width // 2).transpose(0, 2, 1, 3)
    return packed.reshape(expert_count, 2 * slots, width // 2), mixing


def shards(
    prefill_rows,
    proj_weight,
    latent_gain,
    prefill_position,
    row_owner,
    row_request,
    latent_cache,
    cache_len,
    queries,
    decode_rows,
    moe_gain,
    routes,
    gate_scores,
    gate_weight,
    up_weight,
    down_weight,
):
    ep_count = lax.axis_size("ep")
    pre_count = prefill_rows.shape[0]
    step_count, req_count, width = decode_rows.shape
    latent_width = proj_weight.shape[1]
    expert_count = ep_count // PLANE
    assert MOE_FF == PLANE * gate_weight.shape[1]
    capacity = max(2, req_count * TOP // expert_count)
    assert step_count * capacity * 2 == SLAB

    token_rows = decode_rows.astype(jnp.float32)
    factor = lax.rsqrt(jnp.mean(token_rows * token_rows, axis=2, keepdims=True) + NORM_EPS)
    normed = (token_rows * factor * moe_gain[None, None, :]).astype(jnp.bfloat16)
    packed, mixing = pack(normed, routes, gate_scores, expert_count, capacity)

    projected, back = exchange(
        proj_weight,
        packed,
        prefill_rows,
        decode_rows.reshape(step_count * req_count, width),
        gate_weight,
        up_weight,
        down_weight,
    )

    decode_position = (
        cache_len[None, :] + jnp.arange(step_count, dtype=jnp.int32)[:, None]
    ).reshape(-1)
    positions = jnp.concatenate([prefill_position, decode_position], axis=0)
    latent = latent_rows(projected, positions, latent_gain)
    own_rows = latent[pre_count:].reshape(step_count, req_count, latent_width)
    send_cap = max(2, 2 * pre_count // ep_count)
    payload = jnp.concatenate(
        [latent[:pre_count], (row_request + 1).astype(jnp.bfloat16)[:, None]], axis=1
    )
    placed = place_rows(row_owner[:, 0], payload, ep_count, send_cap)
    received = lax.all_to_all(placed, "ep", split_axis=0, concat_axis=0, tiled=True)
    received = received.reshape(-1, latent_width + 1)
    attn_out = attend(
        queries,
        latent_cache,
        cache_len,
        received[:, :latent_width],
        received[:, latent_width].astype(jnp.int32) - 1,
        own_rows,
    )
    slots = step_count * capacity
    expert_rows = back.reshape(expert_count, 2, slots, width // 2).transpose(0, 2, 1, 3)
    moe_out = jnp.dot(
        mixing,
        expert_rows.reshape(expert_count * slots, width),
        precision=lax.Precision.HIGHEST,
        preferred_element_type=jnp.float32,
    )
    moe_out = moe_out.reshape(step_count, req_count, width).astype(jnp.bfloat16)
    return (attn_out, moe_out)


def solution(mesh):
    in_specs = (
        P(("groups", "ep"), None),
        P("ep", None),
        P(),
        P(("groups", "ep")),
        P(("groups", "ep"), None),
        P(("groups", "ep")),
        P(("groups", "ep"), None, None),
        P(("groups", "ep")),
        P(None, ("groups", "ep"), None, None),
        P(None, ("groups", "ep"), None),
        P(),
        P(None, ("groups", "ep"), None),
        P(None, ("groups", "ep"), None),
        P(None, "ep"),
        P(None, "ep"),
        P("ep", None),
    )
    out_specs = (P(None, ("groups", "ep"), None, None), P(None, ("groups", "ep"), None))
    return jax.shard_map(shards, mesh=mesh, in_specs=in_specs, out_specs=out_specs, check_vma=False)
```

time: 325 us -> 155 us (0.48)
  waiting for transfers between devices: 174 us -> 9.51 us
  Pallas kernels: 0 us -> 116 us
  starting transfers between devices: 39.8 us -> 2.59 us
  local copies, waits for them, and re-layouts: 38.7 us -> 5.99 us
  matrix products: 38.1 us -> 6.6 us
  between operations: 14.6 us -> 0.86 us
  other arithmetic: 17.7 us -> 12.6 us
    all_to_all x9 -> x0, waiting for transfers between devices: 165 us -> none  [the longest x4 116 us: shards(): lax.all_to_all(packed[step_at][0], 'ep', split_axis=0, concat_axis=0, til...]
    pallas_call x0 -> x1, Pallas kernels: none -> 116 us  [exchange(): pl.pallas_call(functools.partial(exchange_kernel, E), out_shape=(jax.Shap...]
    all_to_all x9 -> x0, starting transfers between devices: 35.9 us -> none  [the longest x4 15.2 us: shards(): lax.all_to_all(expert_block(lax.all_to_all(packed[step_at][0], 'ep', spli...]
    dot_general x17 -> x2, matrix products: 28.8 us -> 2.5 us  [the longest x1 1.42 us: shards(): jnp.dot(mixing, expert_rows.reshape(expert_count * slots, width), precisi...]
    reshape x20 -> x1, local copies, waits for them, and re-layouts: 25.2 us -> 0.06 us  [pack(): normed.reshape(-1, width)]
    reduce_sum x11 -> x2, other arithmetic: 8.84 us -> 0.1 us  [the longest x1 0.08 us: pack(): jnp.sum(jnp.where(match, gate_scores.reshape(-1, TOP)[:, :, None], 0.0),...]
    broadcast_in_dim x9 -> x2, local copies, waits for them, and re-layouts: 5.84 us -> 0.22 us  [the longest x1 0.13 us: shards(): (row_request + 1).astype(jnp.bfloat16)[:, None]]
  transfers between devices with their start and end apart: 11 -> 1, of which waited for: 10 -> 1; matrix products, arithmetic and copies ran while one was open for 25% -> 2% of each run, Pallas kernels for 0% -> 0%
where the time goes in v1:
time: 155 us; the launch traced here: 154 us
  Pallas kernels  116 us (75%)
  other arithmetic  12.6 us (8%)
  waiting for transfers between devices  9.51 us (6%)
  matrix products  6.6 us (4%)
  local copies, waits for them, and re-layouts  5.99 us (4%)
  starting transfers between devices  2.59 us (2%)
    pallas_call x1, Pallas kernels, exchange(): pl.pallas_call(functools.partial(exchange_kernel, E), out_shape=(jax.Shap...  116 us
    all_to_all x1, waiting for transfers between devices, shards(): lax.all_to_all(placed, 'ep', split_axis=0, concat_axis=0, tiled=True)  9.51 us
  transfers between devices with their start and end apart: 1, of which 1 were waited for; matrix products, arithmetic and copies ran while one was open for 2% of the time, Pallas kernels for 0%

profile of v1, /device:TPU:0, one launch (start us, length us, event | category | flops | bytes accessed | tf_op | source)
XLA Modules:
  0.0 154.3 jit_solution(5904108632783689215)
XLA Ops:
  0.7 0.9 copy.93
  1.5 0.7 broadcast_multiply_fusion
  2.2 1.2 fusion.24
  3.4 1.7 %reshape.199.dec_ref = bf16[16,7168]{1,0:T(8,128)(2,1)} reshape(bf16[4,4,7168]{2,1,0:T(4,128)(2,1)} %param.25) | data formatting | bytes 458752 | tf_op jit(solution)/shard_map/reshape | solution.py:496
  5.1 0.7 convert_bitcast_fusion
  5.7 0.1 add.110
  5.8 0.1 add.111
  5.9 0.7 iota_add_fusion
  6.6 0.1 add.121
  6.6 0.1 copy.94
  6.7 0.1 mul.125
  6.8 0.7 reduce_window_sum.23
  7.6 0.1 reduce_sum.76
  7.6 0.1 copy.95
  7.7 0.1 fusion.46
  7.8 0.1 copy.97
  7.9 0.7 fusion.39
  8.7 0.2 reduce_window_sum.22
  8.9 0.8 select_reduce_fusion
  9.7 0.7 multiply_add_fusion
  10.4 1.1 fusion.26
  11.5 0.1 reshape.196
  11.6 1.1 convolution_convert_fusion
  12.7 116.2 %shard_map.167 = (f32[144,576]{1,0:T(8,128)}, f32[4,16,3584]{2,1,0:T(8,128)}) custom-call(bf16[224,576]{1,0:T(8,128)(2,1)} %w_ref.1, bf16[4,16,3584]{2,1,0:T(8,128)(2,1)} %bitcast.82, bf16[128,7168]{1,0:T(8,128)(2,1)} %pre_hbm.1, bf16[16,7168]{1,0:T(8,128)(2,1)} %reshape.199.dec_ref, bf16[7168,128]{1,0:T(8,128)(2,1)} %gate_hbm.1, bf16[7168,128]{1,0:T(8,128)(2,1)} %up_hbm.1, ...), custom_call_target="tpu_custom_call" | custom-call | tf_op jit(solution)/shard_map/pallas_call | solution.py:404
  128.9 1.1 multiply_reduce_fusion
  130.0 1.3 fusion.35
  131.3 1.1 multiply_convert_fusion
  132.4 0.1 pad_maximum_fusion
  132.5 0.3 convolution_convert_fusion.2
  132.8 0.9 copy.98
  133.7 2.6 %all-to-all-start = ((bf16[32,8,577]{2,1,0:T(8,128)(2,1)}), bf16[32,8,577]{2,1,0:T(8,128)(2,1)S(1)}, u32[]{:S(2)}, u32[]{:S(2)}) async-start(bf16[32,8,577]{2,1,0:T(8,128)(2,1)} %bitcast.9), calls=%async_computation | async-start | bytes 655360 | tf_op jit(solution)/shard_map/all_to_all | solution.py:513
  136.3 0.1 pad_maximum_fusion.1
  136.4 0.1 broadcast_in_dim.106
  136.5 0.1 select_reduce_fusion.1
  136.6 1.4 convolution_convert_fusion.1
  138.1 0.7 fusion.53
  138.8 9.5 %all-to-all-done = bf16[32,8,577]{2,1,0:T(8,128)(2,1)S(1)} async-done(((bf16[32,8,577]{2,1,0:T(8,128)(2,1)}), bf16[32,8,577]{2,1,0:T(8,128)(2,1)S(1)}, u32[]{:S(2)}, u32[]{:S(2)}) %all-to-all-start) | async-done | bytes 295456 | tf_op jit(solution)/shard_map/all_to_all | solution.py:513
  148.3 0.2 add_reduce_fusion
  148.5 0.1 iota_compare_fusion.5
  148.6 0.7 fusion.55
  149.3 0.6 copy-done.6
  149.8 0.7 fusion.54
  150.5 0.1 fusion.40
  150.6 0.9 fusion.14
  151.6 0.5 fusion.15
  152.1 0.6 fusion.42
  152.7 0.6 fusion
  153.3 1.0 copy.108
  (29 shorter events, 0.2 us)
Async XLA Ops:
  0.6 137.4 %copy-start = (bf16[4,4,64,576]{3,2,1,0:T(8,128)(2,1)S(1)}, bf16[4,4,64,576]{3,2,1,0:T(8,128)(2,1)}, u32[]{:S(2)}) copy-start(bf16[4,4,64,576]{3,2,1,0:T(8,128)(2,1)} %param.24) | copy-start | bytes 3538948
  12.6 117.3 %copy-start.5 = (s32[128]{0:T(128)S(1)}, s32[128]{0:T(128)}, u32[]{:S(2)}) copy-start(s32[128]{0:T(128)} %param.19) | copy-start | bytes 1540
  12.6 118.7 %copy-start.3 = (f32[512]{0:T(512)S(1)}, f32[512]{0:T(512)}, u32[]{:S(2)}) copy-start(f32[512]{0:T(512)} %param.18) | copy-start | bytes 6148
  132.4 4.0 %copy-start.2 = (f32[4,4,2]{1,2,0:T(2,128)S(1)}, f32[4,4,2]{1,2,0:T(2,128)}, u32[]{:S(2)}) copy-start(f32[4,4,2]{1,2,0:T(2,128)} %param.28) | copy-start | bytes 388
  132.5 4.1 %copy-start.1 = (f32[4,16,3584]{2,1,0:T(8,128)S(1)}, f32[4,16,3584]{2,1,0:T(8,128)}, u32[]{:S(2)}) copy-start(f32[4,16,3584]{2,1,0:T(8,128)} %get-tuple-element.5) | copy-start | bytes 2752516
  133.7 14.6 %all-to-all-start = ((bf16[32,8,577]{2,1,0:T(8,128)(2,1)}), bf16[32,8,577]{2,1,0:T(8,128)(2,1)S(1)}, u32[]{:S(2)}, u32[]{:S(2)}) async-start(bf16[32,8,577]{2,1,0:T(8,128)(2,1)} %bitcast.9), calls=%async_computation | async-start | bytes 655360 | tf_op jit(solution)/shard_map/all_to_all | solution.py:513
  136.6 11.9 %copy-start.4 = (s32[4]{0:T(128)S(1)}, s32[4]{0:T(128)}, u32[]{:S(2)}) copy-start(s32[4]{0:T(128)} %param.23) | copy-start | bytes 52
  148.6 1.3 copy-start.6

commit v2 on v1

--- a/solution.py
+++ b/solution.py
@@ -216,48 +216,6 @@
 
         hidden[e] = (jax.nn.silu(joined(0)) * joined(2)).astype(jnp.bfloat16)
 
-    loads[2].wait()
-    loads[3].wait()
-
-    @pl.loop(0, E + 3)
-    def _(t):
-        @pl.when(t < E)
-        def _():
-            e = (e0 + t) % E
-            for kind in (0, 1):
-                @pl.when(t > 0)
-                def _():
-                    column_recv(kind, e).wait_recv()
-                for which in (0, 1, 2):
-                    plane_send(kind, e, which).start()
-
-        @pl.when((t >= 1) & (t < E + 1))
-        def _():
-            e = (e0 + t - 1) % E
-            for kind in (0, 1):
-                plane_recv(kind, e, 0).wait_recv()
-                plane_send(kind, e, 3).start()
-                plane_send(kind, e, 4).start()
-                plane_recv(kind, e, 1).wait_recv()
-                plane_send(kind, e, 5).start()
-
-        @pl.when((t >= 2) & (t < E + 2))
-        def _():
-            e = (e0 + t - 2) % E
-            for kind in (0, 1):
-                plane_recv(kind, e, 3).wait_recv()
-                plane_send(kind, e, 6).start()
-
-        @pl.when(t >= 3)
-        def _():
-            e = (e0 + t - 3) % E
-            for which in (2, 4, 5, 6):
-                plane_recv(0, e, which).wait_recv()
-            expert_in(e)
-
-    loads[4].wait()
-    loads[5].wait()
-
     def project():
         pre_count = pre.shape[0]
         depth = pre.shape[1] // E
@@ -302,33 +260,85 @@
     def wide(ref):
         return ref.astype(jnp.float32)
 
-    @pl.loop(0, E + 3)
+    def spread(kind, e):
+        for which in (0, 1, 2):
+            plane_send(kind, e, which).start()
+
+    def relay(kind, e):
+        plane_recv(kind, e, 0).wait_recv()
+        plane_send(kind, e, 3).start()
+        plane_send(kind, e, 4).start()
+        plane_recv(kind, e, 1).wait_recv()
+        plane_send(kind, e, 5).start()
+
+    def finish(kind, e):
+        plane_recv(kind, e, 3).wait_recv()
+        plane_send(kind, e, 6).start()
+
+    def expert_out(e):
+        @pl.loop(0, half // TILE)
+        def _(c):
+            first = pl.multiple_of(c * TILE, TILE)
+            second = pl.multiple_of(half + c * TILE, TILE)
+            low, high = (
+                jnp.dot(
+                    hidden[e], down[:, pl.ds(start, TILE)],
+                    preferred_element_type=jnp.float32,
+                ).reshape(PLANE, SLAB // 2, TILE)
+                for start in (first, second)
+            )
+            part[e, :, :, pl.ds(first, TILE)] = jnp.concatenate([low, high], axis=1).astype(
+                jnp.bfloat16
+            )
+
+    spread(0, e0)
+    spread(1, e0)
+    loads[2].wait()
+    loads[3].wait()
+    loads[4].wait()
+    loads[5].wait()
+
+    def stage(t, lag, first=0):
+        def wrap(body):
+            k = t - lag
+
+            @pl.when((k >= first) & (k < E))
+            def _():
+                body((e0 + E - k) % E)
+
+        return wrap
+
+    @pl.loop(1, E + 6)
     def _(t):
-        @pl.when(t < E)
-        def _():
-            e = (e0 + 1 + t) % E
-
-            @pl.loop(0, half // TILE)
-            def _(c):
-                first = pl.multiple_of(c * TILE, TILE)
-                second = pl.multiple_of(half + c * TILE, TILE)
-                low, high = (
-                    jnp.dot(
-                        hidden[e], down[:, pl.ds(start, TILE)],
-                        preferred_element_type=jnp.float32,
-                    ).reshape(PLANE, SLAB // 2, TILE)
-                    for start in (first, second)
-                )
-                part[e, :, :, pl.ds(first, TILE)] = jnp.concatenate([low, high], axis=1).astype(
-                    jnp.bfloat16
-                )
-
-            for which in range(4):
+        @stage(t, 0, 1)
+        def _(e):
+            column_recv(0, e).wait_recv()
+            spread(0, e)
+
+        @stage(t, 1)
+        def _(e):
+            relay(0, e)
+
+        @stage(t, 1, 1)
+        def _(e):
+            column_recv(1, e).wait_recv()
+            spread(1, e)
+
+        @stage(t, 2)
+        def _(e):
+            finish(0, e)
+
+        @stage(t, 3)
+        def _(e):
+            for which in (2, 4, 5, 6):
+                plane_recv(0, e, which).wait_recv()
+            expert_in(e)
+            expert_out(e)
+            for which in (1, 3, 2, 0):
                 sib_send(e, which).start()
 
-        @pl.when((t >= 1) & (t < E + 1))
-        def _():
-            e = (e0 + t) % E
+        @stage(t, 4)
+        def _(e):
             sib_send(e, 1).wait_recv()
             sum_a[e] = (wide(part[e, jA]) + wide(from_sib[e, 1])).astype(jnp.bfloat16)
             a_send(e, 0).start()
@@ -336,9 +346,8 @@
             sum_d[e] = (wide(part[e, jD]) + wide(from_sib[e, 3])).astype(jnp.bfloat16)
             a_send(e, 1).start()
 
-        @pl.when((t >= 2) & (t < E + 2))
-        def _():
-            e = (e0 + t - 1) % E
+        @stage(t, 5)
+        def _(e):
             sib_send(e, 0).wait_recv()
             sib_send(e, 2).wait_recv()
             a_send(e, 1).wait_recv()
@@ -349,20 +358,24 @@
             a_send(e, 0).wait_recv()
             own_sum[e] = wide(part[e, j]) + wide(from_sib[e, 0]) + wide(from_a[e, 0])
 
-        @pl.when(t >= 3)
-        def _():
-            e = (e0 + t - 2) % E
+        @stage(t, 6)
+        def _(e):
             b_send(e).wait_recv()
             total[e] = (own_sum[e] + wide(from_b[e])).astype(jnp.bfloat16)
 
-            @pl.when(t < E + 2)
+            @pl.when(t > 6)
             def _():
                 back_send(e).start()
 
-        @pl.when(t == 1)
-        def _():
-            project()
-
+        @stage(t, 4)
+        def _(e):
+            relay(1, e)
+
+        @stage(t, 6)
+        def _(e):
+            finish(1, e)
+
+    project()
     back_ref[e0] = wide(total[e0])
 
     @pl.loop(1, E)

time: 155 us -> 138 us (0.89)
  Pallas kernels: 116 us -> 99.9 us
    pallas_call x1, Pallas kernels: 116 us -> 99.9 us  [exchange(): pl.pallas_call(functools.partial(exchange_kernel, E), out_shape=(jax.Shap...]
where the time goes in v2:
time: 138 us
  Pallas kernels  99.9 us (72%)
  other arithmetic  12.6 us (9%)
  waiting for transfers between devices  9.51 us (7%)
  matrix products  6.59 us (5%)
  local copies, waits for them, and re-layouts  5.99 us (4%)
  starting transfers between devices  2.59 us (2%)
    pallas_call x1, Pallas kernels, exchange(): pl.pallas_call(functools.partial(exchange_kernel, E), out_shape=(jax.Shap...  99.9 us
    all_to_all x1, waiting for transfers between devices, shards(): lax.all_to_all(placed, 'ep', split_axis=0, concat_axis=0, tiled=True)  9.51 us
  transfers between devices with their start and end apart: 1, of which 1 were waited for; matrix products, arithmetic and copies ran while one was open for 2% of the time, Pallas kernels for 0%

profile of v2, /device:TPU:0, one launch (start us, length us, event | category | flops | bytes accessed | tf_op | source)
XLA Modules:
  0.0 138.0 jit_solution(2642430371843220657)
XLA Ops:
  0.7 0.9 copy.93
  1.5 0.7 broadcast_multiply_fusion
  2.2 1.2 fusion.24
  3.4 1.7 %reshape.199.dec_ref = bf16[16,7168]{1,0:T(8,128)(2,1)} reshape(bf16[4,4,7168]{2,1,0:T(4,128)(2,1)} %param.25) | data formatting | bytes 458752 | tf_op jit(solution)/shard_map/reshape | solution.py:509
  5.1 0.7 convert_bitcast_fusion
  5.7 0.1 add.110
  5.8 0.1 add.111
  5.9 0.7 iota_add_fusion
  6.6 0.1 add.121
  6.6 0.1 copy.94
  6.7 0.1 mul.125
  6.8 0.7 reduce_window_sum.23
  7.6 0.1 reduce_sum.76
  7.6 0.1 copy.95
  7.7 0.1 fusion.46
  7.8 0.1 copy.97
  7.9 0.7 fusion.39
  8.7 0.2 reduce_window_sum.22
  8.9 0.8 select_reduce_fusion
  9.7 0.7 multiply_add_fusion
  10.4 1.1 fusion.26
  11.5 0.1 reshape.196
  11.6 1.1 convolution_convert_fusion
  12.7 99.9 %shard_map.167 = (f32[144,576]{1,0:T(8,128)}, f32[4,16,3584]{2,1,0:T(8,128)}) custom-call(bf16[224,576]{1,0:T(8,128)(2,1)} %w_ref.1, bf16[4,16,3584]{2,1,0:T(8,128)(2,1)} %bitcast.82, bf16[128,7168]{1,0:T(8,128)(2,1)} %pre_hbm.1, bf16[16,7168]{1,0:T(8,128)(2,1)} %reshape.199.dec_ref, bf16[7168,128]{1,0:T(8,128)(2,1)} %gate_hbm.1, bf16[7168,128]{1,0:T(8,128)(2,1)} %up_hbm.1, ...), custom_call_target="tpu_custom_call" | custom-call | tf_op jit(solution)/shard_map/pallas_call | solution.py:417
  112.5 1.1 multiply_reduce_fusion
  113.6 1.3 fusion.35
  115.0 1.1 multiply_convert_fusion
  116.0 0.1 pad_maximum_fusion
  116.2 0.3 convolution_convert_fusion.2
  116.5 0.9 copy.98
  117.4 2.6 %all-to-all-start = ((bf16[32,8,577]{2,1,0:T(8,128)(2,1)}), bf16[32,8,577]{2,1,0:T(8,128)(2,1)S(1)}, u32[]{:S(2)}, u32[]{:S(2)}) async-start(bf16[32,8,577]{2,1,0:T(8,128)(2,1)} %bitcast.9), calls=%async_computation | async-start | bytes 655360 | tf_op jit(solution)/shard_map/all_to_all | solution.py:526
  120.0 0.1 pad_maximum_fusion.1
  120.0 0.1 broadcast_in_dim.106
  120.1 0.1 select_reduce_fusion.1
  120.3 1.4 %convolution_convert_fusion.1 = bf16[4,4,7168]{2,1,0:T(4,128)(2,1)} fusion(f32[4,4,32]{2,1,0:T(4,128)S(1)} %bitcast.93, f32[32,7168,1]{1,0,2:T(8,128)S(1)} %bitcast.83), kind=kOutput, calls=%fused_computation.1 | convolution fusion | flops 44154880 | bytes 1148928 | tf_op jit(solution)/shard_map/dot_general | solution.py:538
  121.7 0.7 fusion.53
  122.4 9.5 %all-to-all-done = bf16[32,8,577]{2,1,0:T(8,128)(2,1)S(1)} async-done(((bf16[32,8,577]{2,1,0:T(8,128)(2,1)}), bf16[32,8,577]{2,1,0:T(8,128)(2,1)S(1)}, u32[]{:S(2)}, u32[]{:S(2)}) %all-to-all-start) | async-done | bytes 295456 | tf_op jit(solution)/shard_map/all_to_all | solution.py:526
  131.9 0.2 add_reduce_fusion
  132.1 0.1 iota_compare_fusion.5
  132.2 0.7 fusion.55
  132.9 0.6 copy-done.6
  133.5 0.7 fusion.54
  134.2 0.1 fusion.40
  134.3 0.9 fusion.14
  135.2 0.5 fusion.15
  135.8 0.6 fusion.42
  136.3 0.6 fusion
  136.9 1.0 copy.108
  (29 shorter events, 0.2 us)
Async XLA Ops:
  0.6 121.1 %copy-start = (bf16[4,4,64,576]{3,2,1,0:T(8,128)(2,1)S(1)}, bf16[4,4,64,576]{3,2,1,0:T(8,128)(2,1)}, u32[]{:S(2)}) copy-start(bf16[4,4,64,576]{3,2,1,0:T(8,128)(2,1)} %param.24) | copy-start | bytes 3538948
  12.6 101.0 %copy-start.5 = (s32[128]{0:T(128)S(1)}, s32[128]{0:T(128)}, u32[]{:S(2)}) copy-start(s32[128]{0:T(128)} %param.19) | copy-start | bytes 1540
  12.6 102.3 %copy-start.3 = (f32[512]{0:T(512)S(1)}, f32[512]{0:T(512)}, u32[]{:S(2)}) copy-start(f32[512]{0:T(512)} %param.18) | copy-start | bytes 6148
  116.0 4.0 %copy-start.2 = (f32[4,4,2]{1,2,0:T(2,128)S(1)}, f32[4,4,2]{1,2,0:T(2,128)}, u32[]{:S(2)}) copy-start(f32[4,4,2]{1,2,0:T(2,128)} %param.28) | copy-start | bytes 388
  116.1 4.1 %copy-start.1 = (f32[4,16,3584]{2,1,0:T(8,128)S(1)}, f32[4,16,3584]{2,1,0:T(8,128)}, u32[]{:S(2)}) copy-start(f32[4,16,3584]{2,1,0:T(8,128)} %get-tuple-element.5) | copy-start | bytes 2752516
  117.4 14.6 %all-to-all-start = ((bf16[32,8,577]{2,1,0:T(8,128)(2,1)}), bf16[32,8,577]{2,1,0:T(8,128)(2,1)S(1)}, u32[]{:S(2)}, u32[]{:S(2)}) async-start(bf16[32,8,577]{2,1,0:T(8,128)(2,1)} %bitcast.9), calls=%async_computation | async-start | bytes 655360 | tf_op jit(solution)/shard_map/all_to_all | solution.py:526
  120.3 11.9 %copy-start.4 = (s32[4]{0:T(128)S(1)}, s32[4]{0:T(128)}, u32[]{:S(2)}) copy-start(s32[4]{0:T(128)} %param.23) | copy-start | bytes 52
  132.2 1.3 copy-start.6

commit v3 on v2

--- a/solution.py
+++ b/solution.py
@@ -451,23 +451,27 @@
     )(proj_weight, packed, prefill_rows, decode_flat, gate_weight, up_weight, down_weight)
 
 
-def pack(normed, routes, gate_scores, expert_count, capacity):
-    step_count, req_count, width = normed.shape
+def slot_match(routes, expert_count, capacity):
+    step_count, req_count, _ = routes.shape
     chosen = routes.reshape(step_count, req_count * TOP)
-    onehot = (chosen[:, :, None] == jnp.arange(expert_count, dtype=jnp.int32)).astype(jnp.int32)
-    earlier = jnp.cumsum(onehot, axis=1) - onehot
+    order = jnp.arange(req_count * TOP, dtype=jnp.int32)
+    same = (chosen[:, :, None] == chosen[:, None, :]) & (order[None, :] < order[:, None])
     slots = step_count * capacity
     step_ids = jnp.arange(step_count, dtype=jnp.int32)[:, None]
-    row = chosen * slots + step_ids * capacity + jnp.sum(earlier * onehot, axis=2)
+    row = chosen * slots + step_ids * capacity + jnp.sum(same.astype(jnp.int32), axis=2)
     row = row.reshape(step_count * req_count, TOP)
-    match = row[:, :, None] == jnp.arange(expert_count * slots, dtype=jnp.int32)
-    mixing = jnp.sum(jnp.where(match, gate_scores.reshape(-1, TOP)[:, :, None], 0.0), axis=1)
-    select = jnp.any(match, axis=1).astype(jnp.bfloat16)
+    return row[:, :, None] == jnp.arange(expert_count * slots, dtype=jnp.int32)
+
+
+def pack(normed, routes, expert_count, capacity):
+    width = normed.shape[2]
+    slots = normed.shape[0] * capacity
+    select = jnp.any(slot_match(routes, expert_count, capacity), axis=1).astype(jnp.bfloat16)
     packed = jnp.einsum(
         "tr,td->rd", select, normed.reshape(-1, width), preferred_element_type=jnp.float32
     ).astype(jnp.bfloat16)
     packed = packed.reshape(expert_count, slots, 2, width // 2).transpose(0, 2, 1, 3)
-    return packed.reshape(expert_count, 2 * slots, width // 2), mixing
+    return packed.reshape(expert_count, 2 * slots, width // 2)
 
 
 def shards(
@@ -500,7 +504,7 @@
     token_rows = decode_rows.astype(jnp.float32)
     factor = lax.rsqrt(jnp.mean(token_rows * token_rows, axis=2, keepdims=True) + NORM_EPS)
     normed = (token_rows * factor * moe_gain[None, None, :]).astype(jnp.bfloat16)
-    packed, mixing = pack(normed, routes, gate_scores, expert_count, capacity)
+    packed = pack(normed, routes, expert_count, capacity)
 
     projected, back = exchange(
         proj_weight,
@@ -512,6 +516,7 @@
         down_weight,
     )
 
+    projected, late_routes = lax.optimization_barrier((projected, routes))
     decode_position = (
         cache_len[None, :] + jnp.arange(step_count, dtype=jnp.int32)[:, None]
     ).reshape(-1)
@@ -534,6 +539,8 @@
         own_rows,
     )
     slots = step_count * capacity
+    match = slot_match(late_routes, expert_count, capacity)
+    mixing = jnp.sum(jnp.where(match, gate_scores.reshape(-1, TOP)[:, :, None], 0.0), axis=1)
     expert_rows = back.reshape(expert_count, 2, slots, width // 2).transpose(0, 2, 1, 3)
     moe_out = jnp.dot(
         mixing,

time: 138 us -> 138 us (level)
    another operation x3 -> x2, other arithmetic: 3.08 us -> 2.36 us
where the time goes in v3:
time: 138 us; the launch traced here: 137 us
  Pallas kernels  99.9 us (72%)
  other arithmetic  12.4 us (9%)
  waiting for transfers between devices  8.83 us (6%)
  matrix products  6.6 us (5%)
  local copies, waits for them, and re-layouts  6.32 us (5%)
  starting transfers between devices  2.59 us (2%)
    pallas_call x1, Pallas kernels, exchange(): pl.pallas_call(functools.partial(exchange_kernel, E), out_shape=(jax.Shap...  99.9 us
    all_to_all x1, waiting for transfers between devices, shards(): lax.all_to_all(placed, 'ep', split_axis=0, concat_axis=0, tiled=True)  8.83 us
  transfers between devices with their start and end apart: 1, of which 1 were waited for; matrix products, arithmetic and copies ran while one was open for 2% of the time, Pallas kernels for 0%

profile of v3, /device:TPU:0, one launch (start us, length us, event | category | flops | bytes accessed | tf_op | source)
XLA Modules:
  0.0 137.5 jit_solution(2417068658516243146)
XLA Ops:
  0.7 0.8 broadcast_multiply_fusion.1
  1.5 0.8 copy.120
  2.2 1.2 fusion.24
  3.4 1.7 %reshape.240.dec_ref = bf16[16,7168]{1,0:T(8,128)(2,1)} reshape(bf16[4,4,7168]{2,1,0:T(4,128)(2,1)} %param.25) | data formatting | bytes 458752 | tf_op jit(solution)/shard_map/reshape | solution.py:513
  5.1 0.7 convert_bitcast_fusion
  5.8 0.1 add.134
  5.9 0.7 iota_add_fusion
  6.6 0.1 add.144
  6.7 0.1 mul.131
  6.7 0.1 copy.121
  6.8 0.2 convert_reduce_fusion.1
  7.0 0.1 reduce_sum.87
  7.1 0.1 copy.123
  7.2 0.1 fusion.46
  7.3 0.1 copy.125
  7.4 0.7 fusion.39
  8.2 0.2 reduce_window_sum.11
  8.4 0.8 select_reduce_fusion
  9.2 0.7 multiply_add_fusion
  9.9 1.1 fusion.26
  11.1 1.1 convolution_convert_fusion
  12.1 99.9 %shard_map.167 = (f32[144,576]{1,0:T(8,128)}, f32[4,16,3584]{2,1,0:T(8,128)}) custom-call(bf16[224,576]{1,0:T(8,128)(2,1)} %w_ref.1, bf16[4,16,3584]{2,1,0:T(8,128)(2,1)} %bitcast.85, bf16[128,7168]{1,0:T(8,128)(2,1)} %pre_hbm.1, bf16[16,7168]{1,0:T(8,128)(2,1)} %reshape.240.dec_ref, bf16[7168,128]{1,0:T(8,128)(2,1)} %gate_hbm.1, bf16[7168,128]{1,0:T(8,128)(2,1)} %up_hbm.1, ...), custom_call_target="tpu_custom_call" | custom-call | tf_op jit(solution)/shard_map/pallas_call | solution.py:417
  112.0 1.1 multiply_reduce_fusion
  113.1 1.3 fusion.35
  114.4 1.1 multiply_convert_fusion
  115.5 0.1 pad_maximum_fusion
  115.7 0.3 convolution_convert_fusion.2
  115.9 0.9 copy.126
  116.8 2.6 %all-to-all-start = ((bf16[32,8,577]{2,1,0:T(8,128)(2,1)}), bf16[32,8,577]{2,1,0:T(8,128)(2,1)S(1)}, u32[]{:S(2)}, u32[]{:S(2)}) async-start(bf16[32,8,577]{2,1,0:T(8,128)(2,1)} %bitcast.9), calls=%async_computation | async-start | bytes 655360 | tf_op jit(solution)/shard_map/all_to_all | solution.py:531
  119.5 0.1 copy.136
  119.6 0.1 broadcast_in_dim.113
  119.7 0.1 copy.137
  119.8 0.2 convert_reduce_fusion
  120.0 0.1 mul.156
  120.2 0.1 copy.139
  120.4 1.4 %convolution_convert_fusion.1 = bf16[4,4,7168]{2,1,0:T(4,128)(2,1)} fusion(f32[4,4,32]{2,1,0:T(4,128)S(1)} %bitcast.96, f32[32,7168,1]{1,0,2:T(8,128)S(1)} %bitcast.86), kind=kOutput, calls=%fused_computation.1 | convolution fusion | flops 44154880 | bytes 1148928 | tf_op jit(solution)/shard_map/dot_general | solution.py:545
  121.9 0.7 fusion.52
  122.6 8.8 %all-to-all-done = bf16[32,8,577]{2,1,0:T(8,128)(2,1)S(1)} async-done(((bf16[32,8,577]{2,1,0:T(8,128)(2,1)}), bf16[32,8,577]{2,1,0:T(8,128)(2,1)S(1)}, u32[]{:S(2)}, u32[]{:S(2)}) %all-to-all-start) | async-done | bytes 295456 | tf_op jit(solution)/shard_map/all_to_all | solution.py:531
  131.4 0.2 add_reduce_fusion
  131.7 0.7 fusion.54
  132.4 0.6 copy-done.7
  133.0 0.7 fusion.53
  133.7 0.1 fusion.40
  133.8 0.9 fusion.14
  134.7 0.5 fusion.15
  135.3 0.6 fusion.42
  135.8 0.6 fusion
  136.4 1.0 copy.141
  (39 shorter events, 0.6 us)
Async XLA Ops:
  0.6 121.2 %copy-start = (bf16[4,4,64,576]{3,2,1,0:T(8,128)(2,1)S(1)}, bf16[4,4,64,576]{3,2,1,0:T(8,128)(2,1)}, u32[]{:S(2)}) copy-start(bf16[4,4,64,576]{3,2,1,0:T(8,128)(2,1)} %param.24) | copy-start | bytes 3538948
  12.1 101.0 %copy-start.6 = (s32[128]{0:T(128)S(1)}, s32[128]{0:T(128)}, u32[]{:S(2)}) copy-start(s32[128]{0:T(128)} %param.19) | copy-start | bytes 1540
  12.1 102.3 %copy-start.4 = (f32[512]{0:T(512)S(1)}, f32[512]{0:T(512)}, u32[]{:S(2)}) copy-start(f32[512]{0:T(512)} %param.18) | copy-start | bytes 6148
  115.5 3.9 %copy-start.2 = (s32[4,4,2]{1,2,0:T(2,128)S(1)}, s32[4,4,2]{1,2,0:T(2,128)}, u32[]{:S(2)}) copy-start(s32[4,4,2]{1,2,0:T(2,128)} %param.27) | copy-start | bytes 388
  115.5 4.1 %copy-start.3 = (f32[4,4,2]{1,2,0:T(2,128)S(1)}, f32[4,4,2]{1,2,0:T(2,128)}, u32[]{:S(2)}) copy-start(f32[4,4,2]{1,2,0:T(2,128)} %param.28) | copy-start | bytes 388
  115.6 4.8 %copy-start.1 = (f32[4,16,3584]{2,1,0:T(8,128)S(1)}, f32[4,16,3584]{2,1,0:T(8,128)}, u32[]{:S(2)}) copy-start(f32[4,16,3584]{2,1,0:T(8,128)} %get-tuple-element.9) | copy-start | bytes 2752516
  116.8 14.6 %all-to-all-start = ((bf16[32,8,577]{2,1,0:T(8,128)(2,1)}), bf16[32,8,577]{2,1,0:T(8,128)(2,1)S(1)}, u32[]{:S(2)}, u32[]{:S(2)}) async-start(bf16[32,8,577]{2,1,0:T(8,128)(2,1)} %bitcast.9), calls=%async_computation | async-start | bytes 655360 | tf_op jit(solution)/shard_map/all_to_all | solution.py:531
  120.4 11.2 %copy-start.5 = (s32[4]{0:T(128)S(1)}, s32[4]{0:T(128)}, u32[]{:S(2)}) copy-start(s32[4]{0:T(128)} %param.23) | copy-start | bytes 52
  131.7 1.3 copy-start.7
